TPU v7x, 32 devices: a whole 2x2x4 slice. The times are simulated.
32 devices in a mesh: seq: 8 (over z, y), head: 4 (over x, core).
Axes of the slice: x: 2, y: 2, z: 4, core: 2. Of those that a mesh axis runs over, the one named last changes fastest.
Arguments:
- tokens: bfloat16 [2, 4096, 1024], P(None, 'seq'), may hold values from -6 to 6
- norm_gain: bfloat16 [1024], P('seq'), may hold values from 0.5 to 1.5
- qk_proj: bfloat16 [1024, 2, 8, 128], P('seq', None, 'head'), may hold values from -0.1875 to 0.1875
- vg_proj: bfloat16 [1024, 2, 8, 256], P('seq', None, 'head'), may hold values from -0.1875 to 0.1875
- ab_proj: bfloat16 [1024, 2, 8], P('seq', None, 'head'), may hold values from -0.1875 to 0.1875
- qk_conv: bfloat16 [4, 2, 8, 128], P(None, None, 'head', 'seq'), may hold values from -3 to 3
- v_conv: bfloat16 [4, 8, 256], P(None, 'head', 'seq'), may hold values from -3 to 3
- decay_terms: float32 [2, 8], P(None, 'head'), may hold values from -9 to 1, as said below
- out_gain: bfloat16 [256], P('seq'), may hold values from 0.5 to 1.5
- out_proj: bfloat16 [8, 256, 1024], P('head', None, 'seq'), may hold values from -0.1875 to 0.1875
- ffn_gain: bfloat16 [1024], P('seq'), may hold values from 0.5 to 1.5
- gate_up: bfloat16 [1024, 2, 2816], P('seq', None, 'head'), may hold values from -0.1875 to 0.1875
- down_proj: bfloat16 [2816, 1024], P('head', 'seq'), may hold values from -0.21875 to 0.21875
- cotangent: bfloat16 [2, 4096, 1024], P(None, 'seq'), may hold values from -6 to 6
Outputs:
- block_out: bfloat16 [2, 4096, 1024], P(None, 'seq')
- tokens_grad: float32 [2, 4096, 1024], P(None, 'seq')
- norm_gain_grad: float32 [1024], P('seq')
- qk_proj_grad: float32 [1024, 2, 8, 128], P('seq', None, 'head')
- vg_proj_grad: float32 [1024, 2, 8, 256], P('seq', None, 'head')
- ab_proj_grad: float32 [1024, 2, 8], P('seq', None, 'head')
- qk_conv_grad: float32 [4, 2, 8, 128], P(None, None, 'head', 'seq')
- v_conv_grad: float32 [4, 8, 256], P(None, 'head', 'seq')
- decay_grad: float32 [2, 8], P(None, 'head')
- out_gain_grad: float32 [256], P('seq')
- out_proj_grad: float32 [8, 256, 1024], P('head', None, 'seq')
- ffn_gain_grad: float32 [1024], P('seq')
- gate_up_grad: float32 [1024, 2, 2816], P('seq', None, 'head')
- down_proj_grad: float32 [2816, 1024], P('head', 'seq')
Inputs may be any that keep to these rules, and one draw needn't show every extreme that they name: decay_terms row 0 lies in -1 to 1 and row 1 in -9 to -3.
All inputs are finite; a program needn't handle non-finite values.
Results may differ from a plain program's by a relative error of at most 0.011.
Values may be sent and summed in bfloat16 or wider, within the bound.
A program may use at most 256 MiB of HBM per device.

v0:
```python
import jax
import jax.numpy as jnp
from jax import lax
from jax.sharding import PartitionSpec as P

SPAN = 64


HIGHEST = lax.Precision.HIGHEST


def from_behind(x, axis, by):
    peers = lax.axis_size(axis)
    pairs = [(i, i + by) for i in range(peers) if 0 <= i + by < peers]
    return lax.ppermute(x, axis, pairs)


def prefix_2(x, axis, combine, identity, reverse):
    peers, mine = (lax.axis_size(axis), lax.axis_index(axis))
    everything = jax.tree.map(lambda part: lax.all_gather(part, axis), x)
    start = jax.tree.map(
        lambda part, zero: jnp.broadcast_to(jnp.asarray(zero, part.dtype), part.shape), x, identity
    )

    def step(k, before):
        at = peers - 1 - k if reverse else k
        reached = at > mine if reverse else at < mine
        new = combine(before, jax.tree.map(lambda part: part[at], everything))
        return jax.tree.map(lambda a, b: jnp.where(reached, a, b), new, before)

    return lax.fori_loop(0, peers, step, start)


def product(first_op, second_op):
    return jnp.matmul(first_op, second_op, precision=HIGHEST)


def flip(matrix):
    return jnp.swapaxes(matrix, -1, -2)


def inverse_unit(strict):
    span_len = strict.shape[-1]
    identity = jnp.eye(span_len, dtype=jnp.float32)
    inverse = identity - strict
    powered = strict
    reached = 2
    while reached < span_len:
        powered = product(powered, powered)
        inverse = product(inverse, identity + powered)
        reached = reached * 2
    return inverse


def span_parts(queries, key_rows, value_rows, beta_rows, log_decay):
    span_len = queries.shape[-2]
    cumulative = jnp.cumsum(log_decay, -1)
    spread = cumulative[..., :, None] - cumulative[..., None, :]
    lower_tri = jnp.tril(jnp.ones((span_len, span_len), jnp.float32))
    below_diag = lower_tri - jnp.eye(span_len, dtype=jnp.float32)
    ratios = lower_tri * jnp.exp(jnp.where(lower_tri > 0, spread, 0.0))
    key_gram = product(key_rows, flip(key_rows))
    strict = beta_rows[..., :, None] * ratios * key_gram * below_diag
    inverse = inverse_unit(strict)
    decayed = jnp.exp(cumulative)
    writes = product(inverse, (beta_rows * decayed)[..., None] * key_rows)
    pseudo = product(inverse, beta_rows[..., None] * value_rows)
    scores = ratios * product(queries, flip(key_rows))
    intra_out = product(scores, pseudo)
    read_map = decayed[..., None] * queries - product(scores, writes)
    tail_decay = jnp.exp(cumulative[..., -1:] - cumulative)
    tail_keys = tail_decay[..., None] * key_rows
    key_eye = jnp.eye(key_rows.shape[-1], dtype=jnp.float32)
    carry_map = decayed[..., -1][..., None, None] * key_eye - product(flip(tail_keys), writes)
    carry_add = product(flip(tail_keys), pseudo)
    return (carry_map, carry_add, read_map, intra_out)


def conv_valid(extended, weights):
    tap_count = weights.shape[0]
    seq_len = extended.shape[1] - tap_count + 1
    summed = weights[0] * extended[:, 0:seq_len]
    for tap_idx in range(1, tap_count):
        summed = summed + weights[tap_idx] * extended[:, tap_idx : tap_idx + seq_len]
    return summed


def unit_rows(values):
    return values * lax.rsqrt(jnp.sum(values * values, -1, keepdims=True) + 1e-06)


def normalize(values, gain_vec, epsilon):
    return values * lax.rsqrt(jnp.mean(values * values, -1, keepdims=True) + epsilon) * gain_vec


def input_norm(values, gain_vec):
    return normalize(values, gain_vec, 1e-06)


def output_norm(mixer_out, gate_pre, gain_vec):
    return normalize(mixer_out, gain_vec, 1e-05) * jax.nn.silu(gate_pre)


def swiglu(gu_pre):
    return jax.nn.silu(gu_pre[:, :, 0]) * gu_pre[:, :, 1]


def mixer_inputs(qk_ext, v_ext, ab_pre, qk_taps, v_taps, decay_terms):
    qk_act = jax.nn.silu(conv_valid(qk_ext, qk_taps))
    queries = unit_rows(qk_act[:, :, 0]) * qk_act.shape[-1] ** (-0.5)
    key_rows = unit_rows(qk_act[:, :, 1])
    value_rows = jax.nn.silu(conv_valid(v_ext, v_taps))
    beta_rows = jax.nn.sigmoid(ab_pre[:, :, 1])
    log_decay = -jnp.exp(decay_terms[0]) * jax.nn.softplus(ab_pre[:, :, 0] + decay_terms[1])
    return (queries, key_rows, value_rows, beta_rows, log_decay)


def to_spans(tensor):
    shaped = tensor.reshape((tensor.shape[0], tensor.shape[1] // SPAN, SPAN) + tensor.shape[2:])
    return jnp.moveaxis(shaped, 3, 1)


def from_spans(tensor):
    shaped = jnp.moveaxis(tensor, 1, 3)
    return shaped.reshape((shaped.shape[0], shaped.shape[1] * shaped.shape[2]) + shaped.shape[3:])


def prepare(qk_ext, v_ext, ab_pre, qk_taps, v_taps, decay_terms):
    queries, key_rows, value_rows, beta_rows, log_decay = mixer_inputs(
        qk_ext, v_ext, ab_pre, qk_taps, v_taps, decay_terms
    )
    return span_parts(
        to_spans(queries),
        to_spans(key_rows),
        to_spans(value_rows),
        to_spans(beta_rows),
        to_spans(log_decay),
    )


def finish(span_terms, state_in):
    carry_map, carry_add, read_map, intra_out = span_terms
    carried = state_in
    states = []
    for span_idx in range(carry_map.shape[2]):
        states.append(carried)
        carried = product(carry_map[:, :, span_idx], carried) + carry_add[:, :, span_idx]
    stacked = jnp.stack(states, 2)
    return (from_spans(intra_out + product(read_map, stacked)), carried)


def compose(span_terms):
    carry_map, carry_add = (span_terms[0], span_terms[1])
    whole_map = carry_map[:, :, 0]
    whole_add = carry_add[:, :, 0]
    for span_idx in range(1, carry_map.shape[2]):
        whole_map = product(carry_map[:, :, span_idx], whole_map)
        whole_add = product(carry_map[:, :, span_idx], whole_add) + carry_add[:, :, span_idx]
    return (whole_map, whole_add)


def chain(earlier_pair, later_pair):
    return (
        product(later_pair[0], earlier_pair[0]),
        product(later_pair[0], earlier_pair[1]) + later_pair[1],
    )


def head_total(values):
    return lax.psum(values, "head")


def per_device(
    tokens,
    norm_gain,
    qk_proj,
    vg_proj,
    ab_proj,
    qk_conv,
    v_conv,
    decay_terms,
    out_gain,
    out_proj,
    ffn_gain,
    gate_up,
    down_proj,
    cotangent,
):
    gathered = (
        lax.all_gather(norm_gain, "seq", axis=0, tiled=True),
        lax.all_gather(qk_proj, "seq", axis=0, tiled=True),
        lax.all_gather(vg_proj, "seq", axis=0, tiled=True),
        lax.all_gather(ab_proj, "seq", axis=0, tiled=True),
        lax.all_gather(qk_conv, "seq", axis=3, tiled=True),
        lax.all_gather(v_conv, "seq", axis=2, tiled=True),
        lax.all_gather(out_gain, "seq", axis=0, tiled=True),
        lax.all_gather(out_proj, "seq", axis=2, tiled=True),
        lax.all_gather(ffn_gain, "seq", axis=0, tiled=True),
        lax.all_gather(gate_up, "seq", axis=0, tiled=True),
        lax.all_gather(down_proj, "seq", axis=1, tiled=True),
    )
    (
        norm_full,
        qk_full,
        vg_full,
        ab_full,
        qkc_full,
        vc_full,
        outg_full,
        outp_full,
        ffng_full,
        gu_full,
        down_full,
    ) = gathered
    tap_count = qk_conv.shape[0]
    edge_len = tap_count - 1
    norm_float = norm_full.astype(jnp.float32)
    tok_float = tokens.astype(jnp.float32)
    seq_len = tok_float.shape[1]
    cot_float = cotangent.astype(jnp.float32)
    normed, pull_first = jax.vjp(input_norm, tok_float, norm_float)
    normed_low = normed.astype(jnp.bfloat16)
    qk_pre = jnp.einsum("bld,dphe->blphe", normed_low, qk_full, preferred_element_type=jnp.float32)
    vg_pre = jnp.einsum("bld,dphe->blphe", normed_low, vg_full, preferred_element_type=jnp.float32)
    ab_pre = jnp.einsum("bld,dph->blph", normed_low, ab_full, preferred_element_type=jnp.float32)
    edge_qk, edge_v = from_behind(
        (qk_pre[:, seq_len - edge_len :], vg_pre[:, seq_len - edge_len :, 0]), "seq", 1
    )
    qk_ext = jnp.concatenate([edge_qk, qk_pre], 1)
    v_ext = jnp.concatenate([edge_v, vg_pre[:, :, 0]], 1)
    span_terms, pull_prepare = jax.vjp(
        prepare,
        qk_ext,
        v_ext,
        ab_pre,
        qkc_full.astype(jnp.float32),
        vc_full.astype(jnp.float32),
        decay_terms,
    )
    whole_map, whole_add = compose(span_terms)
    eye_map = jnp.broadcast_to(jnp.eye(whole_map.shape[-1], dtype=jnp.float32), whole_map.shape)
    zero_add = jnp.zeros_like(whole_add)
    prefix = prefix_2((whole_map, whole_add), "seq", chain, (eye_map, zero_add), False)
    mixer_pair, pull_finish = jax.vjp(finish, span_terms, prefix[1])
    mixer_out = mixer_pair[0]
    gated_out, pull_gate = jax.vjp(
        output_norm, mixer_out, vg_pre[:, :, 1], outg_full.astype(jnp.float32)
    )
    gated_low = gated_out.astype(jnp.bfloat16)
    mix_terms = jnp.einsum(
        "blhe,hed->bld", gated_low, outp_full, preferred_element_type=jnp.float32
    )
    hidden_res = tok_float + head_total(mix_terms)
    normed_ffn, pull_second = jax.vjp(input_norm, hidden_res, ffng_full.astype(jnp.float32))
    normed_ffn_low = normed_ffn.astype(jnp.bfloat16)
    gu_pre = jnp.einsum(
        "bld,dpf->blpf", normed_ffn_low, gu_full, preferred_element_type=jnp.float32
    )
    activated, pull_swiglu = jax.vjp(swiglu, gu_pre)
    activated_low = activated.astype(jnp.bfloat16)
    ffn_terms = jnp.einsum(
        "blf,fd->bld", activated_low, down_full, preferred_element_type=jnp.float32
    )
    block_out = (hidden_res + head_total(ffn_terms)).astype(jnp.bfloat16)
    act_grad = jnp.einsum("bld,fd->blf", cotangent, down_full, preferred_element_type=jnp.float32)
    down_grad = jnp.einsum(
        "blf,bld->fd", activated_low, cotangent, preferred_element_type=jnp.float32
    )
    gu_grad_pre = pull_swiglu(act_grad)[0]
    gu_grad_low = gu_grad_pre.astype(jnp.bfloat16)
    gu_grad = jnp.einsum(
        "bld,blpf->dpf", normed_ffn_low, gu_grad_low, preferred_element_type=jnp.float32
    )
    ffn_norm_terms = jnp.einsum(
        "blpf,dpf->bld", gu_grad_low, gu_full, preferred_element_type=jnp.float32
    )
    ffn_norm_grad = head_total(ffn_norm_terms)
    hidden_from_norm, ffn_gain_grad = pull_second(ffn_norm_grad)
    hidden_grad = cot_float + hidden_from_norm
    mix_grad_low = hidden_grad.astype(jnp.bfloat16)
    gated_grad = jnp.einsum(
        "bld,hed->blhe", mix_grad_low, outp_full, preferred_element_type=jnp.float32
    )
    outp_grad = jnp.einsum(
        "blhe,bld->hed", gated_low, mix_grad_low, preferred_element_type=jnp.float32
    )
    mixer_grad, gate_grad, out_gain_part = pull_gate(gated_grad)
    carry_map, read_map = (span_terms[0], span_terms[2])
    span_grads = to_spans(mixer_grad)
    state_grad = zero_add
    for span_idx in range(carry_map.shape[2] - 1, -1, -1):
        state_grad = product(flip(read_map[:, :, span_idx]), span_grads[:, :, span_idx]) + product(
            flip(carry_map[:, :, span_idx]), state_grad
        )
    suffix = prefix_2((flip(whole_map), state_grad), "seq", chain, (eye_map, zero_add), True)
    terms_grad, state_in_grad = pull_finish((mixer_grad, suffix[1]))
    qk_ext_grad, v_ext_grad, ab_grad_pre, qk_conv_grad, v_conv_grad, decay_part = pull_prepare(
        terms_grad
    )
    back_qk, back_v = from_behind((qk_ext_grad[:, :edge_len], v_ext_grad[:, :edge_len]), "seq", -1)
    qk_pre_grad = qk_ext_grad[:, edge_len:].at[:, seq_len - edge_len :].add(back_qk)
    v_pre_grad = v_ext_grad[:, edge_len:].at[:, seq_len - edge_len :].add(back_v)
    qk_grad_low = qk_pre_grad.astype(jnp.bfloat16)
    vg_grad_low = jnp.stack([v_pre_grad, gate_grad], 2).astype(jnp.bfloat16)
    ab_grad_low = ab_grad_pre.astype(jnp.bfloat16)
    normed_part = jnp.einsum(
        "blphe,dphe->bld", qk_grad_low, qk_full, preferred_element_type=jnp.float32
    )
    normed_part = normed_part + jnp.einsum(
        "blphe,dphe->bld", vg_grad_low, vg_full, preferred_element_type=jnp.float32
    )
    normed_part = normed_part + jnp.einsum(
        "blph,dph->bld", ab_grad_low, ab_full, preferred_element_type=jnp.float32
    )
    normed_grad, out_gain_sum = head_total((normed_part, out_gain_part))
    tok_from_norm, norm_gain_grad = pull_first(normed_grad)
    tokens_grad = hidden_grad + tok_from_norm
    qk_grad = jnp.einsum(
        "bld,blphe->dphe", normed_low, qk_grad_low, preferred_element_type=jnp.float32
    )
    vg_grad = jnp.einsum(
        "bld,blphe->dphe", normed_low, vg_grad_low, preferred_element_type=jnp.float32
    )
    ab_grad = jnp.einsum(
        "bld,blph->dph", normed_low, ab_grad_low, preferred_element_type=jnp.float32
    )
    decay_grad = lax.psum(decay_part, "seq")
    reduced = (
        lax.psum_scatter(norm_gain_grad, "seq", scatter_dimension=0, tiled=True),
        lax.psum_scatter(qk_grad, "seq", scatter_dimension=0, tiled=True),
        lax.psum_scatter(vg_grad, "seq", scatter_dimension=0, tiled=True),
        lax.psum_scatter(ab_grad, "seq", scatter_dimension=0, tiled=True),
        lax.psum_scatter(qk_conv_grad, "seq", scatter_dimension=3, tiled=True),
        lax.psum_scatter(v_conv_grad, "seq", scatter_dimension=2, tiled=True),
        lax.psum_scatter(out_gain_sum, "seq", scatter_dimension=0, tiled=True),
        lax.psum_scatter(outp_grad, "seq", scatter_dimension=2, tiled=True),
        lax.psum_scatter(ffn_gain_grad, "seq", scatter_dimension=0, tiled=True),
        lax.psum_scatter(gu_grad, "seq", scatter_dimension=0, tiled=True),
        lax.psum_scatter(down_grad, "seq", scatter_dimension=1, tiled=True),
    )
    return (
        block_out,
        tokens_grad,
        reduced[0],
        reduced[1],
        reduced[2],
        reduced[3],
        reduced[4],
        reduced[5],
        decay_grad,
        reduced[6],
        reduced[7],
        reduced[8],
        reduced[9],
        reduced[10],
    )


def solution(mesh):
    placed = (
        P(None, "seq", None),
        P("seq"),
        P("seq", None, "head", None),
        P("seq", None, "head", None),
        P("seq", None, "head"),
        P(None, None, "head", "seq"),
        P(None, "head", "seq"),
        P(None, "head"),
        P("seq"),
        P("head", None, "seq"),
        P("seq"),
        P("seq", None, "head"),
        P("head", "seq"),
        P(None, "seq", None),
    )
    return jax.shard_map(
        per_device,
        mesh=mesh,
        in_specs=placed,
        out_specs=(
            P(None, "seq", None),
            P(None, "seq", None),
            P("seq"),
            P("seq", None, "head", None),
            P("seq", None, "head", None),
            P("seq", None, "head"),
            P(None, None, "head", "seq"),
            P(None, "head", "seq"),
            P(None, "head"),
            P("seq"),
            P("head", None, "seq"),
            P("seq"),
            P("seq", None, "head"),
            P("head", "seq"),
        ),
        check_vma=False,
    )
```

profile of v0, /device:TPU:0, one launch (start us, length us, event | category | flops | bytes accessed | tf_op | source)
XLA Modules:
  0.0 1664.2 jit_solution(6782354149008375190)
XLA Ops:
  13.0 22.2 %all-gather.4 = bf16[8,1,128]{2,1,0:T(2,128)(2,1)S(1)} all-gather(bf16[1,1,128]{2,1,0:T(2,128)(2,1)S(1)} %bitcast.923), channel_id=1, replica_groups=mesh['seq'=8,'head'=4] {'seq'}, dimensions={0}, use_global_device_ids=true | all-gather | bytes 2304 | tf_op jit(solution)/shard_map/all_gather | solution.py:190
  35.3 30.8 %all_gather.59 = bf16[4,2,2,128]{0,2,1,3:T(2,128)(2,1)S(1)} all-gather(bf16[4,2,2,16]{0,2,1,3:T(2,128)(2,1)S(1)} %copy.261), channel_id=1, replica_groups=mesh['seq'=8,'head'=4] {'seq'}, dimensions={3}, use_global_device_ids=true | all-gather | bytes 4608 | tf_op jit(solution)/shard_map/all_gather | solution.py:194
  67.3 16.4 all_gather.58
  85.8 31.1 %all_gather.61 = bf16[4,2,256]{0,1,2:T(2,128)(2,1)S(1)} all-gather(bf16[4,2,32]{0,1,2:T(2,128)(2,1)S(1)} %copy.268), channel_id=1, replica_groups=mesh['seq'=8,'head'=4] {'seq'}, dimensions={2}, use_global_device_ids=true | all-gather | bytes 4608 | tf_op jit(solution)/shard_map/all_gather | solution.py:195
  188.6 22.1 %all-reduce.42 = bf16[256]{0:T(256)(128)(2,1)S(1)} all-reduce(bf16[256]{0:T(256)(128)(2,1)S(1)} %dynamic-update-slice.7), channel_id=1, replica_groups=mesh['seq'=8,'head'=4] {'seq'}, use_global_device_ids=true, to_apply=%add.42 | all-reduce | flops 256 | bytes 1024
  220.5 67.2 %all-gather.28.cloned.1.call-done = f32[16,2,128,256]{3,2,1,0:T(8,128)} async-done(((f32[2,2,128,256]{3,2,1,0:T(8,128)}), f32[16,2,128,256]{3,2,1,0:T(8,128)}) %all-gather.28.cloned.1.call-update) | async-done | bytes 4194320 | tf_op jit(solution)/shard_map/all_gather | solution.py:20
  287.6 28.7 %while.32 = (s32[]{:T(128)}, f32[2,2,128,256]{3,2,1,0:T(8,128)}, s32[]{:T(128)}, f32[8,2,2,128,128]{4,3,2,1,0:T(8,128)}, f32[8,2,2,128,256]{4,3,2,1,0:T(8,128)}, /*index=5*/s32[]{:T(128)}, s32[]{:T(128)}) while((s32[]{:T(128)}, f32[2,2,128,256]{3,2,1,0:T(8,128)}, s32[]{:T(128)}, f32[8,2,2,128,128]{4,3,2,1,0:T(8,128)}, ...), condition=%wide.region_5.6_spmd.clone, body=%wide.region_4.5_spmd.clone.sunk | while | flops 201850880 | bytes 3410527 | solution.py:31
  339.9 17.8 %all-gather.5 = bf16[8,1,128]{2,1,0:T(2,128)(2,1)S(1)} all-gather(bf16[1,1,128]{2,1,0:T(2,128)(2,1)S(1)} %bitcast.924), channel_id=1, replica_groups=mesh['seq'=8,'head'=4] {'seq'}, dimensions={0}, use_global_device_ids=true | all-gather | bytes 2304 | tf_op jit(solution)/shard_map/all_gather | solution.py:198
  357.7 64.5 %all-reduce.52.cloned.1.call-done = f32[2,512,1024]{2,1,0:T(8,128)} async-done(((f32[2,512,1024]{2,1,0:T(8,128)}), f32[2,512,1024]{2,1,0:T(8,128)}) %all-reduce.52.cloned.1.call-update) | async-done | bytes 4194320 | tf_op jit(solution)/shard_map/psum | solution.py:170
  427.6 57.0 %all-gather.22.cloned.1.call-done = bf16[1024,2,704]{0,2,1:T(8,128)(2,1)} async-done(((bf16[128,2,704]{0,2,1:T(8,128)(2,1)}), bf16[1024,2,704]{0,2,1:T(8,128)(2,1)}) %all-gather.22.cloned.1.call-update) | async-done | bytes 2883600 | tf_op jit(solution)/shard_map/all_gather | solution.py:199
  484.6 8.8 fusion.38
  493.4 35.5 %all-gather.24.cloned.1.call-done = bf16[704,1024]{1,0:T(8,128)(2,1)} async-done(((bf16[704,128]{1,0:T(8,128)(2,1)}), bf16[704,1024]{1,0:T(8,128)(2,1)}) %all-gather.24.cloned.1.call-update) | async-done | bytes 1441808 | tf_op jit(solution)/shard_map/all_gather | solution.py:200
  528.9 7.6 multiply_bitcast_fusion
  547.4 80.7 %all-reduce.54.cloned.1.call-done = f32[2,512,1024]{2,1,0:T(8,128)} async-done(((f32[2,512,1024]{2,1,0:T(8,128)}), f32[2,512,1024]{2,1,0:T(8,128)}) %all-reduce.54.cloned.1.call-update) | async-done | bytes 4194320 | tf_op jit(solution)/shard_map/psum | solution.py:170
  655.6 5.7 fusion.103
  681.2 73.1 %all-gather.32.cloned.1.call-done = f32[16,2,128,256]{3,2,1,0:T(8,128)} async-done(((f32[2,2,128,256]{3,2,1,0:T(8,128)}), f32[16,2,128,256]{3,2,1,0:T(8,128)}) %all-gather.32.cloned.1.call-update) | async-done | bytes 4194320 | tf_op jit(solution)/shard_map/all_gather | solution.py:20
  754.2 28.9 %while.33 = (s32[]{:T(128)}, f32[2,2,128,256]{3,2,1,0:T(8,128)}, s32[]{:T(128)}, f32[8,2,2,128,128]{4,3,2,1,0:T(8,128)}, f32[8,2,2,128,256]{4,3,2,1,0:T(8,128)},...) while((s32[]{:T(128)}, f32[2,2,128,256]{3,2,1,0:T(8,128)}, s32[]{:T(128)}, ...), condition=%wide.region_14.15_spmd.clone, body=%wide.region_13.14_spmd.clone.sunk | while | flops 201850880 | bytes 3410589 | solution.py:31
  866.5 5.7 fusion.131
  872.6 6.2 multiply_select_fusion
  937.6 5.7 convolution_bitcast_fusion.1
  955.6 9.6 convolution_bitcast_fusion
  968.3 44.1 %reduce-scatter.27.cloned.1.call-done = f32[16,16]{1,0:T(8,128)} async-done(((f32[128,16]{1,0:T(8,128)}), f32[16,16]{1,0:T(8,128)}) %reduce-scatter.27.cloned.1.call-update) | async-done | bytes 1040
  1014.0 63.2 %reduce-scatter.25.cloned.1.call-done = f32[128,4]{1,0:T(8,128)} async-done(((f32[1024,4]{1,0:T(8,128)}), f32[128,4]{1,0:T(8,128)}) %reduce-scatter.25.cloned.1.call-update) | async-done | bytes 2064
  1078.7 153.4 %all-reduce.56.cloned.1.call-done = (f32[2,512,1024]{2,1,0:T(8,128)}, f32[2,512,1024]{2,1,0:T(8,128)}) async-done(((f32[2,512,1024]{2,1,0:T(8,128)}, f32[2,512,1024]{2,1,0:T(8,128)}), (f32[2,512,1024]{2,1,0:T(8,128)}, f32[2,512,1024]{2,1,0:T(8,128)})) %all-reduce.56.cloned.1.call-update) | async-done | bytes 8388624 | tf_op jit(solution)/shard_map/psum | solution.py:170
  1235.8 37.3 %all-reduce.46 = (f32[1024]{0:T(1024)S(1)}, f32[2,2]{1,0:T(2,128)}, f32[256]{0:T(256)S(1)}, f32[1024]{0:T(1024)S(1)}) all-reduce(f32[1024]{0:T(1024)S(1)} %get-tuple-element.372, f32[2,2]{1,0:T(2,128)S(1)} %pad_add_fusion.8, f32[256]{0:T(256)S(1)} %copy-done.187, ...), channel_id=6, replica_groups=mesh['seq'=8,'head'=4] {'seq'}, use_global_device_ids=true, to_apply=%region_30.31.clone | all-reduce | flops 2308 | bytes 18464
  1274.3 30.6 %reduce-scatter.15.cloned.1.call-done = f32[128,2,2,128]{3,0,2,1:T(8,128)} async-done(((f32[1024,2,2,128]{3,0,2,1:T(8,128)}), f32[128,2,2,128]{3,0,2,1:T(8,128)}) %reduce-scatter.15.cloned.1.call-update) | async-done | bytes 262160 | tf_op jit(solution)/shard_map/reduce_scatter | solution.py:330
  1306.8 6.1 psum.48
  1312.9 6.0 add_convert_fusion.1
  1322.6 73.6 %reduce-scatter.17.cloned.1.call-done = f32[128,2,2,256]{3,0,2,1:T(8,128)} async-done(((f32[1024,2,2,256]{3,0,2,1:T(8,128)}), f32[128,2,2,256]{3,0,2,1:T(8,128)}) %reduce-scatter.17.cloned.1.call-update) | async-done | bytes 524304 | tf_op jit(solution)/shard_map/reduce_scatter | solution.py:331
  1398.4 73.8 %reduce-scatter.23.cloned.1.call-done = f32[704,128]{1,0:T(8,128)} async-done(((f32[704,1024]{1,0:T(8,128)}), f32[704,128]{1,0:T(8,128)}) %reduce-scatter.23.cloned.1.call-update) | async-done | bytes 360464 | tf_op jit(solution)/shard_map/reduce_scatter | solution.py:339
  1472.2 71.5 %reduce-scatter.19.cloned.1.call-done = f32[2,256,128]{2,1,0:T(8,128)} async-done(((f32[2,256,1024]{2,1,0:T(8,128)}), f32[2,256,128]{2,1,0:T(8,128)}) %reduce-scatter.19.cloned.1.call-update) | async-done | bytes 262160 | tf_op jit(solution)/shard_map/reduce_scatter | solution.py:336
  1543.7 113.4 %reduce-scatter.21.cloned.1.call-done = f32[128,2,704]{0,2,1:T(8,128)} async-done(((f32[1024,2,704]{0,2,1:T(8,128)}), f32[128,2,704]{0,2,1:T(8,128)}) %reduce-scatter.21.cloned.1.call-update) | async-done | bytes 720912 | tf_op jit(solution)/shard_map/reduce_scatter | solution.py:338
  (715 shorter events, 403.7 us)
Async XLA Ops:
  7.2 112.6 %all-gather.16.cloned.1.call-start = ((), (), s32[]{:S(2)}) async-start(), calls=%async_computation.8 | async-start | bytes 1179648 | tf_op jit(solution)/shard_map/all_gather | solution.py:191
  8.8 154.6 %all-gather.18.cloned.1.call-start = ((), (), s32[]{:S(2)}) async-start(), calls=%async_computation.9 | async-start | bytes 2359296 | tf_op jit(solution)/shard_map/all_gather | solution.py:192
  10.6 209.9 %all-gather.26.cloned.1.call-start = ((), (), s32[]{:S(2)}) async-start(), calls=%async_computation.20 | async-start | bytes 2359296 | tf_op jit(solution)/shard_map/all_gather | solution.py:20
  10.7 132.4 %copy-start.105 = (f32[64,64]{1,0:T(8,128)}, f32[64,64]{1,0:T(8,128)S(1)}, u32[]{:S(2)}) copy-start(f32[64,64]{1,0:T(8,128)S(1)} %fusion.251) | copy-start | bytes 49156
  10.7 144.6 %copy-start.114 = (f32[128,128]{1,0:T(8,128)}, f32[128,128]{1,0:T(8,128)S(1)}, u32[]{:S(2)}) copy-start(f32[128,128]{1,0:T(8,128)S(1)} %fusion.242) | copy-start | bytes 196612
  13.0 106.8 %copy-start.146 = (f32[2,512]{1,0:T(2,128)}, f32[2,512]{1,0:T(2,128)S(1)}, u32[]{:S(2)}) copy-start(f32[2,512]{1,0:T(2,128)S(1)} %fusion.270) | copy-start | bytes 12292
  123.7 9.6 collective-permute-start
  159.6 386.2 %copy-start.1 = (f32[2,2,8,128,128]{4,3,2,1,0:T(8,128)}, f32[2,2,8,128,128]{4,3,2,1,0:T(8,128)S(1)}, u32[]{:S(2)}) copy-start(f32[2,2,8,128,128]{4,3,2,1,0:T(8,128)S(1)} %multiply_subtract_fusion) | copy-start | bytes 6291460
  163.4 124.3 %all-gather.28.cloned.1.call-start = ((), (), s32[]{:S(2)}) async-start(), calls=%async_computation.21 | async-start | bytes 4718592 | tf_op jit(solution)/shard_map/all_gather | solution.py:20
  168.1 4.3 collective-permute-start.1
  186.4 147.1 %all-gather.20.cloned.1.call-start = ((), (), s32[]{:S(2)}) async-start(), calls=%async_computation.10 | async-start | bytes 1179648 | tf_op jit(solution)/shard_map/all_gather | solution.py:197
  187.0 235.2 %all-reduce.52.cloned.1.call-start = ((), (), s32[]{:S(2)}) async-start(), calls=%async_computation.11 | async-start | bytes 8388608 | tf_op jit(solution)/shard_map/psum | solution.py:170
  210.6 119.0 %copy-start.182 = (f32[256]{0:T(256)}, f32[256]{0:T(256)S(1)}, u32[]{:S(2)}) copy-start(f32[256]{0:T(256)S(1)} %convert_element_type.90) | copy-start | bytes 3076
  338.3 146.3 %all-gather.22.cloned.1.call-start = ((), (), s32[]{:S(2)}) async-start(), calls=%async_computation.12 | async-start | bytes 3244032 | tf_op jit(solution)/shard_map/all_gather | solution.py:199
  339.1 189.8 %all-gather.24.cloned.1.call-start = ((), (), s32[]{:S(2)}) async-start(), calls=%async_computation.13 | async-start | bytes 1622016 | tf_op jit(solution)/shard_map/all_gather | solution.py:200
  339.8 288.3 %all-reduce.54.cloned.1.call-start = ((), (), s32[]{:S(2)}) async-start(), calls=%async_computation.14 | async-start | bytes 8388608 | tf_op jit(solution)/shard_map/psum | solution.py:170
  357.7 126.9 %copy-start.150 = (f32[8,1,128]{2,1,0:T(1,128)}, f32[8,1,128]{2,1,0:T(1,128)S(1)}, u32[]{:S(2)}) copy-start(f32[8,1,128]{2,1,0:T(1,128)S(1)} %convert_element_type.102) | copy-start | bytes 12292
  544.1 137.0 %all-gather.30.cloned.1.call-start = ((), (), s32[]{:S(2)}) async-start(), calls=%async_computation.22 | async-start | bytes 2359296 | tf_op jit(solution)/shard_map/all_gather | solution.py:20
  547.3 86.1 %copy-start.151 = (f32[8,1,128]{2,1,0:T(1,128)S(1)}, f32[8,1,128]{2,1,0:T(1,128)}, u32[]{:S(2)}) copy-start(f32[8,1,128]{2,1,0:T(1,128)} %copy-done.150) | copy-start | bytes 12292
  547.4 86.1 %copy-start.154 = (f32[2,512]{1,0:T(2,128)S(1)}, f32[2,512]{1,0:T(2,128)}, u32[]{:S(2)}) copy-start(f32[2,512]{1,0:T(2,128)} %copy-done.153) | copy-start | bytes 12292
  547.4 206.9 %all-gather.32.cloned.1.call-start = ((), (), s32[]{:S(2)}) async-start(), calls=%async_computation.23 | async-start | bytes 4718592 | tf_op jit(solution)/shard_map/all_gather | solution.py:20
  655.1 311.6 %reduce-scatter.29.cloned.1.call-start = ((), (), s32[]{:S(2)}) async-start(), calls=%async_computation.26 | async-start | bytes 147456
  889.4 123.0 %reduce-scatter.27.cloned.1.call-start = ((), (), s32[]{:S(2)}) async-start(), calls=%async_computation.25 | async-start | bytes 73728
  899.0 21.3 %collective-permute-start.3 = (f32[2,3,2,256]{3,1,2,0:T(4,128)S(1)}, f32[2,3,2,256]{3,1,2,0:T(4,128)S(1)}, u32[]{:S(2)}, u32[]{:S(2)}) collective-permute-start(f32[2,3,2,256]{3,1,2,0:T(4,128)S(1)} %pad_add_fusion.4), channel_id=1, source_target_pairs={{4,0},{8,4},{12,8},{16,12},{20,16},{24,20},{28,24},{5,1},{9,5},{13... | collective-permute-start | bytes 36872 | tf_op jit(solution)/shard_map/ppermute | solution.py:15
  911.5 165.7 %reduce-scatter.25.cloned.1.call-start = ((), (), s32[]{:S(2)}) async-start(), calls=%async_computation.24 | async-start | bytes 589824
  917.4 6.3 collective-permute-start.2
  920.3 311.8 %all-reduce.56.cloned.1.call-start = ((), (), s32[]{:S(2)}) async-start(), calls=%async_computation.27 | async-start | bytes 16777216 | tf_op jit(solution)/shard_map/psum | solution.py:170
  932.1 372.8 %reduce-scatter.15.cloned.1.call-start = ((), (), s32[]{:S(2)}) async-start(), calls=%async_computation.15 | async-start | bytes 2359296 | tf_op jit(solution)/shard_map/reduce_scatter | solution.py:330
  936.4 459.7 %reduce-scatter.17.cloned.1.call-start = ((), (), s32[]{:S(2)}) async-start(), calls=%async_computation.16 | async-start | bytes 4718592 | tf_op jit(solution)/shard_map/reduce_scatter | solution.py:331
  943.4 528.8 %reduce-scatter.23.cloned.1.call-start = ((), (), s32[]{:S(2)}) async-start(), calls=%async_computation.19 | async-start | bytes 3244032 | tf_op jit(solution)/shard_map/reduce_scatter | solution.py:339
  948.9 594.8 %reduce-scatter.19.cloned.1.call-start = ((), (), s32[]{:S(2)}) async-start(), calls=%async_computation.17 | async-start | bytes 2359296 | tf_op jit(solution)/shard_map/reduce_scatter | solution.py:336
  954.9 702.2 %reduce-scatter.21.cloned.1.call-start = ((), (), s32[]{:S(2)}) async-start(), calls=%async_computation.18 | async-start | bytes 6488064 | tf_op jit(solution)/shard_map/reduce_scatter | solution.py:338
  (188 other events, 1525.1 us)
Sparse Core Ops, SparseCore 0:
  10.8 43.2 all-gather.15
  56.8 49.1 all-gather.17
  163.5 49.5 all-gather.25
  215.6 71.9 all-gather.27
  289.5 37.7 all-gather.19
  338.5 83.6 all-reduce.51
  424.4 60.1 all-gather.21
  486.9 41.9 all-gather.23
  544.2 83.8 all-reduce.53
  630.7 49.4 all-gather.29
  682.3 71.8 all-gather.31
  889.5 59.1 reduce-scatter.28
  952.1 60.3 reduce-scatter.26
  1016.2 60.9 reduce-scatter.24
  1079.8 152.2 all-reduce.55
  1236.4 68.4 reduce-scatter.14
  1308.8 87.2 reduce-scatter.16
  1400.1 72.0 reduce-scatter.22
  1476.3 67.3 reduce-scatter.18
  1547.8 109.3 reduce-scatter.20
where the time goes:
time: 1670 us; the launch traced here: 1660 us
  waiting for transfers between devices  1010 us (60%)
  matrix products  307 us (18%)
  blocking collectives  184 us (11%)
  local copies, waits for them, and re-layouts  76.9 us (5%)
  other arithmetic  61.9 us (4%)
  between operations  19.6 us (1%)
    psum x3, waiting for transfers between devices, head_total(): return lax.psum(values, 'head')  299 us
    dot_general x125, matrix products, product(): return jnp.matmul(first_op, second_op, precision=HIGHEST)  224 us
    all_gather x4, waiting for transfers between devices, prefix_2(): everything = jax.tree.map(lambda part: lax.all_gather(part, axis), x)  140 us
    reduce_scatter x1, waiting for transfers between devices, per_device(): lax.psum_scatter(gu_grad, 'seq', scatter_dimension=0, tiled=True)  113 us
    unnamed x23, waiting for transfers between devices  110 us
    reduce_scatter x1, waiting for transfers between devices, per_device(): lax.psum_scatter(down_grad, 'seq', scatter_dimension=1, tiled=True)  73.8 us
    reduce_scatter x1, waiting for transfers between devices, per_device(): lax.psum_scatter(vg_grad, 'seq', scatter_dimension=0, tiled=True)  73.6 us
    reduce_scatter x1, waiting for transfers between devices, per_device(): lax.psum_scatter(outp_grad, 'seq', scatter_dimension=2, tiled=True)  71.5 us
  transfers between devices with their start and end apart: 24, of which 16 were waited for; matrix products, arithmetic and copies ran while one was open for 17% of the time, Pallas kernels for 0%

commit v1 on v0

v1 whole, which is shorter than its diff:
```python
import jax
import jax.numpy as jnp
from jax import lax
from jax.sharding import PartitionSpec as P

SPAN = 64


HIGH = lax.Precision.HIGH


def from_behind(x, axis, by):
    peers = lax.axis_size(axis)
    pairs = [(i, i + by) for i in range(peers) if 0 <= i + by < peers]
    return lax.ppermute(x, axis, pairs)


def product(first_op, second_op):
    return jnp.matmul(first_op, second_op, precision=HIGH)


def flip(matrix):
    return jnp.swapaxes(matrix, -1, -2)


def inverse_unit(strict):
    span_len = strict.shape[-1]
    identity = jnp.eye(span_len, dtype=jnp.float32)
    inverse = identity - strict
    powered = strict
    reached = 2
    while reached < span_len:
        powered = product(powered, powered)
        inverse = product(inverse, identity + powered)
        reached = reached * 2
    return inverse


def span_parts(queries, key_rows, value_rows, beta_rows, log_decay):
    span_len = queries.shape[-2]
    cumulative = jnp.cumsum(log_decay, -1)
    spread = cumulative[..., :, None] - cumulative[..., None, :]
    lower_tri = jnp.tril(jnp.ones((span_len, span_len), jnp.float32))
    below_diag = lower_tri - jnp.eye(span_len, dtype=jnp.float32)
    ratios = lower_tri * jnp.exp(jnp.where(lower_tri > 0, spread, 0.0))
    key_gram = product(key_rows, flip(key_rows))
    strict = beta_rows[..., :, None] * ratios * key_gram * below_diag
    inverse = inverse_unit(strict)
    decayed = jnp.exp(cumulative)
    writes = product(inverse, (beta_rows * decayed)[..., None] * key_rows)
    pseudo = product(inverse, beta_rows[..., None] * value_rows)
    scores = ratios * product(queries, flip(key_rows))
    intra_out = product(scores, pseudo)
    read_map = decayed[..., None] * queries - product(scores, writes)
    tail_decay = jnp.exp(cumulative[..., -1:] - cumulative)
    tail_keys = tail_decay[..., None] * key_rows
    key_eye = jnp.eye(key_rows.shape[-1], dtype=jnp.float32)
    carry_map = decayed[..., -1][..., None, None] * key_eye - product(flip(tail_keys), writes)
    carry_add = product(flip(tail_keys), pseudo)
    return (carry_map, carry_add, read_map, intra_out)


def conv_valid(extended, weights):
    tap_count = weights.shape[0]
    seq_len = extended.shape[1] - tap_count + 1
    summed = weights[0] * extended[:, 0:seq_len]
    for tap_idx in range(1, tap_count):
        summed = summed + weights[tap_idx] * extended[:, tap_idx : tap_idx + seq_len]
    return summed


def unit_rows(values):
    return values * lax.rsqrt(jnp.sum(values * values, -1, keepdims=True) + 1e-06)


def normalize(values, gain_vec, epsilon):
    return values * lax.rsqrt(jnp.mean(values * values, -1, keepdims=True) + epsilon) * gain_vec


def input_norm(values, gain_vec):
    return normalize(values, gain_vec, 1e-06)


def output_norm(mixer_out, gate_pre, gain_vec):
    return normalize(mixer_out, gain_vec, 1e-05) * jax.nn.silu(gate_pre)


def swiglu(gu_pre):
    return jax.nn.silu(gu_pre[:, :, 0]) * gu_pre[:, :, 1]


def mixer_inputs(qk_ext, v_ext, ab_pre, qk_taps, v_taps, decay_terms):
    qk_act = jax.nn.silu(conv_valid(qk_ext, qk_taps))
    queries = unit_rows(qk_act[:, :, 0]) * qk_act.shape[-1] ** (-0.5)
    key_rows = unit_rows(qk_act[:, :, 1])
    value_rows = jax.nn.silu(conv_valid(v_ext, v_taps))
    beta_rows = jax.nn.sigmoid(ab_pre[:, :, 1])
    log_decay = -jnp.exp(decay_terms[0]) * jax.nn.softplus(ab_pre[:, :, 0] + decay_terms[1])
    return (queries, key_rows, value_rows, beta_rows, log_decay)


def to_spans(tensor):
    shaped = tensor.reshape((tensor.shape[0], tensor.shape[1] // SPAN, SPAN) + tensor.shape[2:])
    return jnp.moveaxis(shaped, 3, 1)


def from_spans(tensor):
    shaped = jnp.moveaxis(tensor, 1, 3)
    return shaped.reshape((shaped.shape[0], shaped.shape[1] * shaped.shape[2]) + shaped.shape[3:])


def prepare(qk_ext, v_ext, ab_pre, qk_taps, v_taps, decay_terms):
    queries, key_rows, value_rows, beta_rows, log_decay = mixer_inputs(
        qk_ext, v_ext, ab_pre, qk_taps, v_taps, decay_terms
    )
    return span_parts(
        to_spans(queries),
        to_spans(key_rows),
        to_spans(value_rows),
        to_spans(beta_rows),
        to_spans(log_decay),
    )


def finish(span_terms, state_in):
    carry_map, carry_add, read_map, intra_out = span_terms
    carried = state_in
    states = []
    for span_idx in range(carry_map.shape[2]):
        states.append(carried)
        carried = product(carry_map[:, :, span_idx], carried) + carry_add[:, :, span_idx]
    stacked = jnp.stack(states, 2)
    return (from_spans(intra_out + product(read_map, stacked)), carried)


def compose(span_terms):
    carry_map, carry_add = (span_terms[0], span_terms[1])
    whole_map = carry_map[:, :, 0]
    whole_add = carry_add[:, :, 0]
    for span_idx in range(1, carry_map.shape[2]):
        whole_map = product(carry_map[:, :, span_idx], whole_map)
        whole_add = product(carry_map[:, :, span_idx], whole_add) + carry_add[:, :, span_idx]
    return (whole_map, whole_add)


def head_rows(values, count):
    mine = lax.axis_index("head")
    return lax.dynamic_slice_in_dim(values, mine * count, count, 1)


def per_device(
    tokens,
    norm_gain,
    qk_proj,
    vg_proj,
    ab_proj,
    qk_conv,
    v_conv,
    decay_terms,
    out_gain,
    out_proj,
    ffn_gain,
    gate_up,
    down_proj,
    cotangent,
):
    f32, bf16 = jnp.float32, jnp.bfloat16
    peers = lax.axis_size("seq")
    head_peers = lax.axis_size("head")
    rows, width = norm_gain.shape[0], norm_gain.shape[0] * peers
    taps, _, heads, dk_part = qk_conv.shape
    dv_part = v_conv.shape[2]
    dk, dv = qk_proj.shape[3], vg_proj.shape[3]
    hidden = gate_up.shape[2]
    seqs, seq_len = tokens.shape[:2]
    quarter = seq_len // head_peers
    qk_n, vg_n, ab_n = 2 * heads * dk, 2 * heads * dv, 2 * heads

    small = jnp.concatenate([qk_conv.reshape(-1), v_conv.reshape(-1), out_gain])
    small_n = small.shape[0]
    small_cols = -(-small_n // rows)
    small = jnp.pad(small, (0, small_cols * rows - small_n)).reshape(rows, small_cols)
    used = qk_n + vg_n + ab_n + 2 + small_cols
    spare = -used % 128
    first_local = jnp.concatenate(
        [
            qk_proj.reshape(rows, qk_n),
            vg_proj.reshape(rows, vg_n),
            ab_proj.reshape(rows, ab_n),
            norm_gain[:, None],
            ffn_gain[:, None],
            small,
            jnp.zeros((rows, spare), bf16),
        ],
        1,
    )
    first = lax.all_gather(first_local, "seq", axis=0, tiled=True)
    mix_n = heads * dv
    second_local = jnp.concatenate(
        [
            gate_up.reshape(rows, 2 * hidden),
            out_proj.reshape(mix_n, rows).T,
            down_proj.T,
        ],
        1,
    )
    first, second_local = lax.optimization_barrier((first, second_local))
    second = lax.all_gather(second_local, "seq", axis=0, tiled=True)
    gu_full = second[:, : 2 * hidden]
    outp_t = second[:, 2 * hidden : 2 * hidden + mix_n]
    down_t = second[:, 2 * hidden + mix_n :]

    proj_n = qk_n + vg_n + ab_n
    in_proj = first[:, :proj_n]
    norm_float = first[:, proj_n].astype(f32)
    ffng_float = first[:, proj_n + 1].astype(f32)
    small_full = first[:, proj_n + 2 : proj_n + 2 + small_cols].reshape(peers, -1)[:, :small_n]
    qkc_n = taps * 2 * heads * dk_part
    vc_n = taps * heads * dv_part
    qkc_full = jnp.moveaxis(
        small_full[:, :qkc_n].reshape(peers, taps, 2, heads, dk_part), 0, 3
    ).reshape(taps, 2, heads, dk)
    vc_full = jnp.moveaxis(
        small_full[:, qkc_n : qkc_n + vc_n].reshape(peers, taps, heads, dv_part), 0, 2
    ).reshape(taps, heads, dv)
    outg_full = small_full[:, qkc_n + vc_n :].reshape(-1).astype(f32)

    edge_len = taps - 1
    tok_float = tokens.astype(f32)
    tok_rows = head_rows(tokens, quarter).astype(f32)
    cot_rows = head_rows(cotangent, quarter).astype(f32)
    normed_low = input_norm(tok_float, norm_float).astype(bf16)
    pre = jnp.einsum("bld,dn->bln", normed_low, in_proj, preferred_element_type=f32)
    qk_pre = pre[:, :, :qk_n].reshape(seqs, seq_len, 2, heads, dk)
    vg_pre = pre[:, :, qk_n : qk_n + vg_n].reshape(seqs, seq_len, 2, heads, dv)
    ab_pre = pre[:, :, qk_n + vg_n :].reshape(seqs, seq_len, 2, heads)
    edge_n = qk_n + heads * dv
    edge = from_behind(pre[:, seq_len - edge_len :, :edge_n], "seq", 1)
    qk_ext = jnp.concatenate(
        [edge[:, :, :qk_n].reshape(seqs, edge_len, 2, heads, dk), qk_pre], 1
    )
    v_ext = jnp.concatenate(
        [edge[:, :, qk_n:].reshape(seqs, edge_len, heads, dv), vg_pre[:, :, 0]], 1
    )
    span_terms, pull_prepare = jax.vjp(
        prepare, qk_ext, v_ext, ab_pre, qkc_full.astype(f32), vc_full.astype(f32), decay_terms
    )
    whole_map, whole_add = compose(span_terms)
    moved = lax.all_gather(jnp.concatenate([whole_map, whole_add], -1).astype(bf16), "seq")
    moved = moved.astype(f32)
    all_maps, all_adds = moved[..., :dk], moved[..., dk:]
    mine = lax.axis_index("seq")

    def from_first(at, state):
        return jnp.where(at < mine, product(all_maps[at], state) + all_adds[at], state)

    state_in = lax.fori_loop(0, peers - 1, from_first, jnp.zeros_like(whole_add), unroll=peers <= 8)
    mixer_pair, pull_finish = jax.vjp(finish, span_terms, state_in)
    mixer_out = mixer_pair[0]
    gated_out, pull_gate = jax.vjp(output_norm, mixer_out, vg_pre[:, :, 1], outg_full)
    gated_low = gated_out.astype(bf16).reshape(seqs, seq_len, mix_n)
    mix_terms = jnp.einsum("bln,dn->bld", gated_low, outp_t, preferred_element_type=f32)
    mix_rows = lax.psum_scatter(
        mix_terms.astype(bf16), "head", scatter_dimension=1, tiled=True
    )
    hidden_rows = tok_rows + mix_rows.astype(f32)
    normed_ffn, pull_second = jax.vjp(input_norm, hidden_rows, ffng_float)
    normed_ffn_low = lax.all_gather(normed_ffn.astype(bf16), "head", axis=1, tiled=True)
    act_grad = jnp.einsum("bld,df->blf", cotangent, down_t, preferred_element_type=f32)
    gu_pre = jnp.einsum("bld,dn->bln", normed_ffn_low, gu_full, preferred_element_type=f32)
    gu_pre = gu_pre.reshape(seqs, seq_len, 2, hidden)
    activated, pull_swiglu = jax.vjp(swiglu, gu_pre)
    activated_low = activated.astype(bf16)
    gu_grad_low = pull_swiglu(act_grad)[0].astype(bf16).reshape(seqs, seq_len, 2 * hidden)
    ffn_norm_terms = jnp.einsum("bln,dn->bld", gu_grad_low, gu_full, preferred_element_type=f32)
    ffn_norm_rows = lax.psum_scatter(
        ffn_norm_terms.astype(bf16), "head", scatter_dimension=1, tiled=True
    )
    hidden_from_norm, ffn_gain_grad = pull_second(ffn_norm_rows.astype(f32))
    hidden_grad = cot_rows + hidden_from_norm
    mix_grad_low = lax.all_gather(hidden_grad.astype(bf16), "head", axis=1, tiled=True)
    ffn_terms = jnp.einsum("blf,df->bld", activated_low, down_t, preferred_element_type=f32)
    ffn_rows = lax.psum_scatter(
        ffn_terms.astype(bf16), "head", scatter_dimension=1, tiled=True
    )
    block_rows = (hidden_rows + ffn_rows.astype(f32)).astype(bf16)
    block_out = lax.all_gather(block_rows, "head", axis=1, tiled=True)
    down_grad = jnp.einsum("bld,blf->df", cotangent, activated_low, preferred_element_type=f32)
    gu_grad = jnp.einsum("bld,bln->dn", normed_ffn_low, gu_grad_low, preferred_element_type=f32)
    gated_grad = jnp.einsum("bld,dn->bln", mix_grad_low, outp_t, preferred_element_type=f32)
    gated_grad = gated_grad.reshape(seqs, seq_len, heads, dv)
    outp_grad = jnp.einsum("bld,bln->dn", mix_grad_low, gated_low, preferred_element_type=f32)
    second_grad = jnp.concatenate(
        [gu_grad.astype(bf16), outp_grad.astype(bf16), down_grad.astype(bf16)], 1
    )
    second_grad, gated_grad = lax.optimization_barrier((second_grad, gated_grad))
    second_sum = lax.psum_scatter(second_grad, "seq", scatter_dimension=0, tiled=True)
    mixer_grad, gate_grad, out_gain_part = pull_gate(gated_grad)
    carry_map, read_map = (span_terms[0], span_terms[2])
    span_grads = to_spans(mixer_grad)
    read_grads = product(flip(read_map), span_grads)
    state_grad = jnp.zeros_like(whole_add)
    for span_idx in range(carry_map.shape[2] - 1, -1, -1):
        state_grad = read_grads[:, :, span_idx] + product(
            flip(carry_map[:, :, span_idx]), state_grad
        )
    all_grads = lax.all_gather(state_grad.astype(bf16), "seq").astype(f32)

    def from_last(step, state):
        at = peers - 1 - step
        return jnp.where(at > mine, product(flip(all_maps[at]), state) + all_grads[at], state)

    state_out_grad = lax.fori_loop(
        0, peers - 1, from_last, jnp.zeros_like(whole_add), unroll=peers <= 8
    )
    terms_grad, state_in_grad = pull_finish((mixer_grad, state_out_grad))
    qk_ext_grad, v_ext_grad, ab_grad_pre, qk_conv_grad, v_conv_grad, decay_part = pull_prepare(
        terms_grad
    )
    ext_grad = jnp.concatenate(
        [
            qk_ext_grad.reshape(seqs, seq_len + edge_len, qk_n),
            v_ext_grad.reshape(seqs, seq_len + edge_len, heads * dv),
        ],
        2,
    )
    back = from_behind(ext_grad[:, :edge_len], "seq", -1)
    conv_in_grad = ext_grad[:, edge_len:].at[:, seq_len - edge_len :].add(back)
    pre_grad_low = jnp.concatenate(
        [
            conv_in_grad.astype(bf16),
            gate_grad.reshape(seqs, seq_len, heads * dv).astype(bf16),
            ab_grad_pre.reshape(seqs, seq_len, ab_n).astype(bf16),
        ],
        2,
    )
    normed_part = jnp.einsum("bln,dn->bld", pre_grad_low, in_proj, preferred_element_type=f32)
    normed_rows = lax.psum_scatter(
        normed_part.astype(bf16), "head", scatter_dimension=1, tiled=True
    )
    first_grad = jnp.einsum("bld,bln->dn", normed_low, pre_grad_low, preferred_element_type=f32)
    conv_grad = jnp.concatenate(
        [
            jnp.moveaxis(qk_conv_grad.reshape(taps, 2, heads, peers, dk_part), 3, 0).reshape(
                peers, qkc_n
            ),
            jnp.moveaxis(v_conv_grad.reshape(taps, heads, peers, dv_part), 2, 0).reshape(
                peers, vc_n
            ),
        ],
        1,
    )
    conv_n = qkc_n + vc_n
    conv_cols = -(-conv_n // rows)
    conv_grad = jnp.pad(conv_grad, ((0, 0), (0, conv_cols * rows - conv_n)))
    first_grad = jnp.concatenate(
        [
            first_grad.astype(bf16),
            conv_grad.reshape(width, conv_cols).astype(bf16),
            jnp.zeros((width, -(proj_n + conv_cols) % 128), bf16),
        ],
        1,
    )
    first_sum = lax.psum_scatter(first_grad, "seq", scatter_dimension=0, tiled=True).astype(f32)
    _, pull_first = jax.vjp(input_norm, tok_rows, norm_float)
    tok_from_norm, norm_gain_grad = pull_first(normed_rows.astype(f32))
    grad_rows = (hidden_grad + tok_from_norm).astype(bf16)
    tokens_grad = lax.all_gather(grad_rows, "head", axis=1, tiled=True).astype(f32)
    decay_all = lax.dynamic_update_slice(
        jnp.zeros((2, heads * head_peers), f32),
        decay_part,
        (0, lax.axis_index("head") * heads),
    )
    vectors = jnp.concatenate(
        [norm_gain_grad, ffn_gain_grad, out_gain_part, decay_all.reshape(-1)]
    )
    vectors = lax.psum(vectors, ("seq", "head"))
    norm_gain_sum = lax.dynamic_slice_in_dim(vectors, mine * rows, rows, 0)
    ffn_gain_sum = lax.dynamic_slice_in_dim(vectors, width + mine * rows, rows, 0)
    gain_n = out_gain.shape[0]
    out_gain_sum = lax.dynamic_slice_in_dim(vectors, 2 * width + mine * gain_n, gain_n, 0)
    decay_grad = lax.dynamic_slice_in_dim(
        vectors[2 * width + dv :].reshape(2, heads * head_peers),
        lax.axis_index("head") * heads,
        heads,
        1,
    )
    conv_sum = first_sum[:, proj_n : proj_n + conv_cols].reshape(-1)
    second_sum = second_sum.astype(f32)
    return (
        block_out,
        tokens_grad,
        norm_gain_sum,
        first_sum[:, :qk_n].reshape(qk_proj.shape),
        first_sum[:, qk_n : qk_n + vg_n].reshape(vg_proj.shape),
        first_sum[:, qk_n + vg_n : proj_n].reshape(ab_proj.shape),
        conv_sum[:qkc_n].reshape(qk_conv.shape),
        conv_sum[qkc_n:conv_n].reshape(v_conv.shape),
        decay_grad,
        out_gain_sum,
        second_sum[:, 2 * hidden : 2 * hidden + mix_n].T.reshape(out_proj.shape),
        ffn_gain_sum,
        second_sum[:, : 2 * hidden].reshape(gate_up.shape),
        second_sum[:, 2 * hidden + mix_n :].T,
    )


def solution(mesh):
    placed = (
        P(None, "seq", None),
        P("seq"),
        P("seq", None, "head", None),
        P("seq", None, "head", None),
        P("seq", None, "head"),
        P(None, None, "head", "seq"),
        P(None, "head", "seq"),
        P(None, "head"),
        P("seq"),
        P("head", None, "seq"),
        P("seq"),
        P("seq", None, "head"),
        P("head", "seq"),
        P(None, "seq", None),
    )
    return jax.shard_map(
        per_device,
        mesh=mesh,
        in_specs=placed,
        out_specs=(
            P(None, "seq", None),
            P(None, "seq", None),
            P("seq"),
            P("seq", None, "head", None),
            P("seq", None, "head", None),
            P("seq", None, "head"),
            P(None, None, "head", "seq"),
            P(None, "head", "seq"),
            P(None, "head"),
            P("seq"),
            P("head", None, "seq"),
            P("seq"),
            P("seq", None, "head"),
            P("head", "seq"),
        ),
        check_vma=False,
    )
```

time: 1670 us -> 994 us (0.60)
  waiting for transfers between devices: 1010 us -> 509 us
  blocking collectives: 184 us -> 41.7 us
  matrix products: 307 us -> 200 us
  local copies, waits for them, and re-layouts: 76.9 us -> 130 us
  other arithmetic: 61.9 us -> 82.3 us
    psum x3 -> x0, waiting for transfers between devices: 299 us -> none  [head_total(): return lax.psum(values, 'head')]
    reduce_scatter x5, waiting for transfers between devices: 363 us -> 195 us  [the longest x1 104 us: per_device(): lax.psum_scatter(second_grad, 'seq', scatter_dimension=0, tiled=True)]
    all_gather x5 -> x0, blocking collectives: 118 us -> none  [the longest x1 31.1 us: per_device(): lax.all_gather(v_conv, 'seq', axis=2, tiled=True)]
    dot_general x143 -> x127, matrix products: 307 us -> 200 us  [the longest x115 135 us: product(): return jnp.matmul(first_op, second_op, precision=HIGH)]
    unnamed x23 -> x15, waiting for transfers between devices: 110 us -> 37.4 us
    unnamed x2 -> x0, blocking collectives: 59.3 us -> none
    all_gather x9 -> x8, waiting for transfers between devices: 233 us -> 272 us  [the longest x1 66.8 us: per_device(): first = lax.all_gather(first_local, 'seq', axis=0, tiled=True)]
    psum x1, blocking collectives: 6.13 us -> 41.7 us  [per_device(): vectors = lax.psum(vectors, ('seq', 'head'))]
  transfers between devices with their start and end apart: 24 -> 16, of which waited for: 16 -> 14; matrix products, arithmetic and copies ran while one was open for 17% -> 14% of each run, Pallas kernels for 0% -> 0%
where the time goes in v1:
time: 994 us; the launch traced here: 985 us
  waiting for transfers between devices  509 us (51%)
  matrix products  200 us (20%)
  local copies, waits for them, and re-layouts  130 us (13%)
  other arithmetic  82.3 us (8%)
  blocking collectives  41.7 us (4%)
  between operations  16.9 us (2%)
    dot_general x115, matrix products, product(): return jnp.matmul(first_op, second_op, precision=HIGH)  135 us
    reduce_scatter x1, waiting for transfers between devices, per_device(): lax.psum_scatter(second_grad, 'seq', scatter_dimension=0, tiled=True)  104 us
    all_gather x1, waiting for transfers between devices, per_device(): first = lax.all_gather(first_local, 'seq', axis=0, tiled=True)  66.8 us
    all_gather x1, waiting for transfers between devices, per_device(): second = lax.all_gather(second_local, 'seq', axis=0, tiled=True)  53.8 us
    all_gather x1, waiting for transfers between devices, per_device(): lax.all_gather(jnp.concatenate([whole_map, whole_add], -1).astype(bf16),...  43.8 us
    psum x1, blocking collectives, per_device(): vectors = lax.psum(vectors, ('seq', 'head'))  41.7 us
    unnamed x15, waiting for transfers between devices  37.4 us
    all_gather x1, waiting for transfers between devices, per_device(): all_grads = lax.all_gather(state_grad.astype(bf16), 'seq').astype(f32)  36.8 us
  transfers between devices with their start and end apart: 16, of which 14 were waited for; matrix products, arithmetic and copies ran while one was open for 14% of the time, Pallas kernels for 0%

profile of v1, /device:TPU:0, one launch (start us, length us, event | category | flops | bytes accessed | tf_op | source)
XLA Modules:
  0.0 985.4 jit_solution(5138054551584028825)
XLA Ops:
  12.2 5.4 concatenate.52
  19.8 66.8 %all-gather.10.cloned.1.call-done = bf16[1024,1664]{0,1:T(8,128)(2,1)} async-done(((bf16[128,1664]{0,1:T(8,128)(2,1)}), bf16[1024,1664]{0,1:T(8,128)(2,1)}) %all-gather.10.cloned.1.call-update) | async-done | bytes 3407888 | tf_op jit(solution)/shard_map/all_gather | solution.py:197
  88.1 5.6 fusion.14
  105.1 4.9 slice_bitcast_fusion.5
  132.5 5.0 fusion.40
  174.6 43.8 %all-gather.12.cloned.1.call-done = bf16[8,2,2,128,384]{4,3,2,1,0:T(8,128)(2,1)} async-done(((bf16[1,2,2,128,384]{4,3,2,1,0:T(8,128)(2,1)}), bf16[8,2,2,128,384]{4,3,2,1,0:T(8,128)(2,1)}) %all-gather.12.cloned.1.call-update) | async-done | bytes 3145744 | tf_op jit(solution)/shard_map/all_gather | solution.py:249
  237.6 4.5 copy.512
  250.7 4.7 multiply_convert_fusion.1
  255.4 53.8 %all-gather.14.cloned.1.call-done = bf16[1024,2624]{1,0:T(8,128)(2,1)} async-done(((bf16[128,2624]{1,0:T(8,128)(2,1)}), bf16[1024,2624]{1,0:T(8,128)(2,1)}) %all-gather.14.cloned.1.call-update) | async-done | bytes 5373968 | tf_op jit(solution)/shard_map/all_gather | solution.py:208
  313.4 29.7 %reduce-scatter.9.cloned.1.call-done = bf16[2,128,1024]{2,1,0:T(8,128)(2,1)} async-done(((bf16[2,512,1024]{2,1,0:T(8,128)(2,1)}), bf16[2,128,1024]{2,1,0:T(8,128)(2,1)}) %reduce-scatter.9.cloned.1.call-update) | async-done | bytes 524304 | tf_op jit(solution)/shard_map/reduce_scatter | solution.py:263
  346.9 22.7 %all-gather.16.cloned.1.call-done = bf16[2,512,1024]{2,1,0:T(8,128)(2,1)} async-done(((bf16[2,128,1024]{2,1,0:T(8,128)(2,1)}), bf16[2,512,1024]{2,1,0:T(8,128)(2,1)}) %all-gather.16.cloned.1.call-update) | async-done | bytes 2097168 | tf_op jit(solution)/shard_map/all_gather | solution.py:268
  369.6 5.9 fusion.24
  375.5 5.7 fusion.19
  383.3 4.7 fusion.50
  388.1 31.5 %reduce-scatter.13.cloned.1.call-done = bf16[2,128,1024]{2,1,0:T(8,128)(2,1)} async-done(((bf16[2,512,1024]{2,1,0:T(8,128)(2,1)}), bf16[2,128,1024]{2,1,0:T(8,128)(2,1)}) %reduce-scatter.13.cloned.1.call-update) | async-done | bytes 524304 | tf_op jit(solution)/shard_map/reduce_scatter | solution.py:276
  428.4 4.9 fusion.62
  435.9 7.6 bitcast_convert_fusion.1
  443.4 4.4 all-gather.20.cloned.1.call-done
  474.2 5.5 fusion.125
  486.8 36.8 %all-gather.24.cloned.1.call-done = bf16[16,2,128,256]{3,2,1,0:T(8,128)(2,1)} async-done(((bf16[2,2,128,256]{3,2,1,0:T(8,128)(2,1)}), bf16[16,2,128,256]{3,2,1,0:T(8,128)(2,1)}) %all-gather.24.cloned.1.call-update) | async-done | bytes 2097168 | tf_op jit(solution)/shard_map/all_gather | solution.py:307
  622.7 4.5 multiply_reduce_fusion.2
  652.4 6.0 scatter-add.4
  658.4 8.3 fusion.51
  668.1 4.7 convolution_convert_fusion.1
  674.7 7.0 bitcast_convert_fusion
  682.4 13.0 %concatenate.64 = bf16[1024,1664]{0,1:T(8,128)(2,1)S(1)} concatenate(bf16[1024,1540]{0,1:T(8,128)(2,1)} %bitcast_convert_fusion, bf16[1024,4]{0,1:T(4,128)(2,1)S(1)} %copy.599, bf16[1024,120]{0,1:T(8,128)(2,1)} %broadcast_in_dim.202), dimensions={1} | concatenate | bytes 6815744 | tf_op jit(solution)/shard_map/concatenate | solution.py:356
  702.2 29.5 %reduce-scatter.11.cloned.1.call-done = bf16[2,128,1024]{2,1,0:T(8,128)(2,1)} async-done(((bf16[2,512,1024]{2,1,0:T(8,128)(2,1)}), bf16[2,128,1024]{2,1,0:T(8,128)(2,1)}) %reduce-scatter.11.cloned.1.call-update) | async-done | bytes 524304 | tf_op jit(solution)/shard_map/reduce_scatter | solution.py:283
  736.0 41.7 %psum.7 = f32[2320]{0:T(1024)S(1)} all-reduce(f32[2320]{0:T(1024)S(1)} %pad_maximum_fusion.9), channel_id=1, replica_groups=mesh['seq'=8,'head'=4] {'seq','head'}, use_global_device_ids=true, to_apply=%region_31.32 | all-reduce | flops 2320 | bytes 18560 | tf_op jit(solution)/shard_map/psum | solution.py:377
  779.6 35.5 %reduce-scatter.19.cloned.1.call-done = bf16[128,1664]{1,0:T(8,128)(2,1)} async-done(((bf16[1024,1664]{1,0:T(8,128)(2,1)}), bf16[128,1664]{1,0:T(8,128)(2,1)}) %reduce-scatter.19.cloned.1.call-update) | async-done | bytes 426000
  820.5 104.2 %reduce-scatter.17.cloned.1.call-done = bf16[128,2624]{1,0:T(8,128)(2,1)} async-done(((bf16[1024,2624]{1,0:T(8,128)(2,1)}), bf16[128,2624]{1,0:T(8,128)(2,1)}) %reduce-scatter.17.cloned.1.call-update) | async-done | bytes 671760 | tf_op jit(solution)/shard_map/reduce_scatter | solution.py:297
  928.9 19.7 %all-gather.18.cloned.1.call-done = bf16[2,512,1024]{2,1,0:T(8,128)(2,1)} async-done(((bf16[2,128,1024]{2,1,0:T(8,128)(2,1)}), bf16[2,512,1024]{2,1,0:T(8,128)(2,1)}) %all-gather.18.cloned.1.call-update) | async-done | bytes 2097168 | tf_op jit(solution)/shard_map/all_gather | solution.py:287
  948.6 24.6 %all-gather.22.cloned.1.call-done = bf16[2,512,1024]{2,1,0:T(8,128)(2,1)} async-done(((bf16[2,128,1024]{2,1,0:T(8,128)(2,1)}), bf16[2,512,1024]{2,1,0:T(8,128)(2,1)}) %all-gather.22.cloned.1.call-update) | async-done | bytes 2097168 | tf_op jit(solution)/shard_map/all_gather | solution.py:368
  (654 shorter events, 315.8 us)
Async XLA Ops:
  7.2 79.3 %all-gather.10.cloned.1.call-start = ((), (), s32[]{:S(2)}) async-start(), calls=%async_computation.6 | async-start | bytes 3833856 | tf_op jit(solution)/shard_map/all_gather | solution.py:197
  17.6 200.7 %all-gather.12.cloned.1.call-start = ((), (), s32[]{:S(2)}) async-start(), calls=%async_computation.7 | async-start | bytes 3538944 | tf_op jit(solution)/shard_map/all_gather | solution.py:249
  18.2 107.2 %copy-start.94 = (f32[64,64]{1,0:T(8,128)}, f32[64,64]{1,0:T(8,128)S(1)}, u32[]{:S(2)}) copy-start(f32[64,64]{1,0:T(8,128)S(1)} %fusion.224) | copy-start | bytes 49156
  18.3 129.5 %copy-start.98 = (f32[128,128]{1,0:T(8,128)}, f32[128,128]{1,0:T(8,128)S(1)}, u32[]{:S(2)}) copy-start(f32[128,128]{1,0:T(8,128)S(1)} %fusion.215) | copy-start | bytes 196612
  18.3 81.2 %copy-start.149 = (f32[2]{0:T(128)}, f32[2]{0:T(128)S(1)}, u32[]{:S(2)}) copy-start(f32[2]{0:T(128)S(1)} %get-tuple-element.186) | copy-start | bytes 28
  18.3 81.1 %copy-start.151 = (f32[2]{0:T(128)}, f32[2]{0:T(128)S(1)}, u32[]{:S(2)}) copy-start(f32[2]{0:T(128)S(1)} %get-tuple-element.187) | copy-start | bytes 28
  18.8 74.8 %copy-start.153 = (f32[2,512]{1,0:T(2,128)}, f32[2,512]{1,0:T(2,128)S(1)}, u32[]{:S(2)}) copy-start(f32[2,512]{1,0:T(2,128)S(1)} %add_rsqrt_fusion.2) | copy-start | bytes 12292
  87.3 334.9 %copy-start.110 = (f32[1024,1]{0,1:T(1,128)}, f32[1024,1]{0,1:T(1,128)S(1)}, u32[]{:S(2)}) copy-start(f32[1024,1]{0,1:T(1,128)S(1)} %get-tuple-element.141) | copy-start | bytes 12292
  101.8 11.1 %collective-permute-start = (f32[2,3,1024]{2,0,1:T(2,128)S(1)}, f32[2,3,1024]{2,0,1:T(2,128)S(1)}, u32[]{:S(2)}, u32[]{:S(2)}) collective-permute-start(f32[2,3,1024]{2,0,1:T(2,128)S(1)} %copy.488), channel_id=1, source_target_pairs={{0,4},{4,8},{8,12},{12,16},{16,20},{20,24},{24,28},{1,5},{5,9},{9,... | collective-permute-start | bytes 73736 | tf_op jit(solution)/shard_map/ppermute | solution.py:15
  110.2 33.4 %copy-start.103 = (f32[2,2,8,64]{3,2,1,0:T(8,128)}, f32[2,2,8,64]{3,2,1,0:T(8,128)S(1)}, u32[]{:S(2)}) copy-start(f32[2,2,8,64]{3,2,1,0:T(8,128)S(1)} %get-tuple-element.176) | copy-start | bytes 24580
  159.5 149.7 %all-gather.14.cloned.1.call-start = ((), (), s32[]{:S(2)}) async-start(), calls=%async_computation.8 | async-start | bytes 6193152 | tf_op jit(solution)/shard_map/all_gather | solution.py:208
  160.3 182.9 %reduce-scatter.9.cloned.1.call-start = ((), (), s32[]{:S(2)}) async-start(), calls=%async_computation.9 | async-start | bytes 2621440 | tf_op jit(solution)/shard_map/reduce_scatter | solution.py:263
  313.4 56.2 %all-gather.16.cloned.1.call-start = ((), (), s32[]{:S(2)}) async-start(), calls=%async_computation.10 | async-start | bytes 2621440 | tf_op jit(solution)/shard_map/all_gather | solution.py:268
  344.6 77.7 %copy-start.125 = (f32[2,128]{1,0:T(2,128)}, f32[2,128]{1,0:T(2,128)S(1)}, u32[]{:S(2)}) copy-start(f32[2,128]{1,0:T(2,128)S(1)} %fusion.244) | copy-start | bytes 3076
  346.8 72.8 %reduce-scatter.13.cloned.1.call-start = ((), (), s32[]{:S(2)}) async-start(), calls=%async_computation.13 | async-start | bytes 2621440 | tf_op jit(solution)/shard_map/reduce_scatter | solution.py:276
  388.1 59.7 %all-gather.20.cloned.1.call-start = ((), (), s32[]{:S(2)}) async-start(), calls=%async_computation.14 | async-start | bytes 2621440 | tf_op jit(solution)/shard_map/all_gather | solution.py:281
  425.0 98.6 %all-gather.24.cloned.1.call-start = ((), (), s32[]{:S(2)}) async-start(), calls=%async_computation.18 | async-start | bytes 2359296 | tf_op jit(solution)/shard_map/all_gather | solution.py:307
  474.2 225.8 %reduce-scatter.15.cloned.1.call-start = ((), (), s32[]{:S(2)}) async-start(), calls=%async_computation.15 | async-start | bytes 2621440 | tf_op jit(solution)/shard_map/reduce_scatter | solution.py:338
  643.7 5.7 collective-permute-start.1
  666.8 64.9 %reduce-scatter.11.cloned.1.call-start = ((), (), s32[]{:S(2)}) async-start(), calls=%async_computation.11 | async-start | bytes 2621440 | tf_op jit(solution)/shard_map/reduce_scatter | solution.py:283
  672.8 142.3 %reduce-scatter.19.cloned.1.call-start = ((), (), s32[]{:S(2)}) async-start(), calls=%async_computation.19 | async-start | bytes 3833856
  699.0 32.7 %copy-start.44 = (bf16[2,128,1024]{2,1,0:T(8,128)(2,1)S(1)}, bf16[2,128,1024]{2,1,0:T(8,128)(2,1)}, u32[]{:S(2)}) copy-start(bf16[2,128,1024]{2,1,0:T(8,128)(2,1)} %reduce-scatter.9.cloned.1.call-done) | copy-start | bytes 1572868
  699.0 32.7 %copy-start.66 = (bf16[2,128,1024]{2,1,0:T(8,128)(2,1)S(1)}, bf16[2,128,1024]{2,1,0:T(8,128)(2,1)}, u32[]{:S(2)}) copy-start(bf16[2,128,1024]{2,1,0:T(8,128)(2,1)} %reduce-scatter.13.cloned.1.call-done) | copy-start | bytes 1572868
  699.0 32.7 %copy-start.111 = (f32[1024,1]{0,1:T(1,128)S(1)}, f32[1024,1]{0,1:T(1,128)}, u32[]{:S(2)}) copy-start(f32[1024,1]{0,1:T(1,128)} %copy-done.110) | copy-start | bytes 12292
  699.0 32.7 %copy-start.126 = (f32[2,128]{1,0:T(2,128)S(1)}, f32[2,128]{1,0:T(2,128)}, u32[]{:S(2)}) copy-start(f32[2,128]{1,0:T(2,128)} %copy-done.125) | copy-start | bytes 3076
  699.1 32.7 %copy-start.147 = (f32[2,128]{1,0:T(2,128)S(1)}, f32[2,128]{1,0:T(2,128)}, u32[]{:S(2)}) copy-start(f32[2,128]{1,0:T(2,128)} %copy-done.146) | copy-start | bytes 3076
  699.1 225.6 %reduce-scatter.17.cloned.1.call-start = ((), (), s32[]{:S(2)}) async-start(), calls=%async_computation.17 | async-start | bytes 6193152 | tf_op jit(solution)/shard_map/reduce_scatter | solution.py:297
  699.7 249.0 %all-gather.18.cloned.1.call-start = ((), (), s32[]{:S(2)}) async-start(), calls=%async_computation.12 | async-start | bytes 2621440 | tf_op jit(solution)/shard_map/all_gather | solution.py:287
  702.1 33.3 %copy-start.108 = (f32[2,8,64,2]{2,1,3,0:T(8,128)S(1)}, f32[2,8,64,2]{2,1,3,0:T(8,128)}, u32[]{:S(2)}) copy-start(f32[2,8,64,2]{2,1,3,0:T(8,128)} %copy-done.107) | copy-start | bytes 24580
  702.2 33.5 %copy-start.156 = (f32[2,2]{1,0:T(2,128)S(1)}, f32[2,2]{1,0:T(2,128)}, u32[]{:S(2)}) copy-start(f32[2,2]{1,0:T(2,128)} %param.23) | copy-start | bytes 52
  702.2 33.8 %copy-start.145 = (f32[1024]{0:T(1024)S(1)}, f32[1024]{0:T(1024)}, u32[]{:S(2)}) copy-start(f32[1024]{0:T(1024)} %get-tuple-element.113) | copy-start | bytes 12292
  734.9 238.4 %all-gather.22.cloned.1.call-start = ((), (), s32[]{:S(2)}) async-start(), calls=%async_computation.16 | async-start | bytes 2621440 | tf_op jit(solution)/shard_map/all_gather | solution.py:368
  (144 other events, 564.1 us)
Sparse Core Ops, SparseCore 0:
  17.7 68.7 all-gather.9
  159.6 58.6 all-gather.11
  221.1 88.0 all-gather.13
  313.5 29.5 reduce-scatter.8
  346.9 22.5 all-gather.15
  388.2 31.4 reduce-scatter.12
  425.1 22.5 all-gather.19
  474.3 49.2 all-gather.23
  666.9 30.7 reduce-scatter.14
  700.3 31.4 reduce-scatter.10
  735.9 79.1 reduce-scatter.18
  819.0 105.6 reduce-scatter.16
  926.2 22.3 all-gather.17
  950.6 22.5 all-gather.21
